TPU v7x, 32 devices: a whole 2x2x4 slice. The times are simulated.
32 devices in a mesh: groups: 2 (over y), var: 8 (over z, x), tm: 2 (over core).
Axes of the slice: x: 2, y: 2, z: 4, core: 2. Of those that a mesh axis runs over, the one named last changes fastest.
Arguments:
- series: bfloat16 [4, 512, 4096], P('groups', 'var', 'tm'), parts along dimension 0, may hold values from -71 to 71
- target: float32 [4, 512, 720], P('groups', 'var', 'tm'), parts along dimension 0, may hold values from -71 to 71
- w_embed: bfloat16 [4096, 512], P('tm'), may hold values from -0.09375 to 0.09375
- w_query: bfloat16 [512, 256], P(None, 'tm'), may hold values from -0.25 to 0.25
- w_key: bfloat16 [512, 256], P(None, 'tm'), may hold values from -0.25 to 0.25
- w_value: bfloat16 [512, 256], P(None, 'tm'), may hold values from -0.25 to 0.25
- w_out: bfloat16 [256, 512], P('tm'), may hold values from -0.375 to 0.375
- norm_gain: float32 [512], replicated, may hold values from 0.5 to 1.5
- w_head: bfloat16 [512, 720], P(None, 'tm'), may hold values from -0.25 to 0.25
Outputs:
- predicted_values: float32 [4, 512, 720], P('groups', 'var', 'tm'), parts along dimension 0
- question_projection_derivative: float32 [1024, 256], P('groups', 'tm'), parts along dimension 0
- final_projection_derivative: float32 [512, 512], P(('groups', 'tm')), parts along dimension 0
- layernorm_scale_derivative: float32 [1024], P('groups'), parts along dimension 0
- future_readout_derivative: float32 [1024, 720], P('groups', 'tm'), parts along dimension 0
There are 2 independent parts, one for each index of `groups`. A program takes and returns all parts, laid end to end along the dimension named above; an argument that names none is the same for every part. Nothing has to cross between parts.
All inputs are finite; a program needn't handle non-finite values.
Results may differ from a plain program's by a relative error of at most 0.015.
Values may be sent and summed in bfloat16 or wider, within the bound.
A program may use at most 128 MiB of HBM per device.

v0:
```python
import jax
import jax.numpy as jnp
from jax import lax
from jax.sharding import PartitionSpec as P

HEAD_DIM = 64
HOR = 720
SAMPLES = 2
epsilon = 1e-05


def split_heads(tensor_in):
    return tensor_in.reshape(tensor_in.shape[:-1] + (tensor_in.shape[-1] // HEAD_DIM, HEAD_DIM))


def project(inputs, matrix):
    return jnp.einsum("svd,da->sva", inputs, matrix, preferred_element_type=jnp.float32).astype(
        jnp.bfloat16
    )


def forward_attend(queries, key_rows, value_rows):
    scores = jnp.einsum(
        "nhe,mhe->hnm", queries, key_rows, preferred_element_type=jnp.float32
    ) * HEAD_DIM ** (-0.5)
    powers = jnp.exp(scores)
    row_sums = jnp.sum(powers, axis=2)
    summed = jnp.einsum(
        "hnm,mhe->nhe", powers.astype(jnp.bfloat16), value_rows, preferred_element_type=jnp.float32
    )
    return (summed / jnp.transpose(row_sums)[:, :, None], row_sums)


def attend_all(queries, key_rows, value_rows):
    contexts = []
    totals = []
    for sample in range(queries.shape[0]):
        context, row_sums = forward_attend(
            split_heads(queries[sample]),
            split_heads(key_rows[sample]),
            split_heads(value_rows[sample]),
        )
        contexts.append(context.reshape(queries.shape[1], queries.shape[2]))
        totals.append(row_sums)
    return (jnp.stack(contexts), totals)


def backward_attend(queries, key_rows, value_rows, row_sums, context, grad_context):
    scores = jnp.einsum(
        "nhe,mhe->hnm", queries, key_rows, preferred_element_type=jnp.float32
    ) * HEAD_DIM ** (-0.5)
    weights = jnp.exp(scores) / row_sums[:, :, None]
    grad_weights = jnp.einsum(
        "nhe,mhe->hnm",
        grad_context.astype(jnp.bfloat16),
        value_rows,
        preferred_element_type=jnp.float32,
    )
    row_dots = jnp.sum(grad_context * context, axis=2)
    grad_scores = (weights * (grad_weights - jnp.transpose(row_dots)[:, :, None])).astype(
        jnp.bfloat16
    )
    return jnp.einsum(
        "hnm,mhe->nhe", grad_scores, key_rows, preferred_element_type=jnp.float32
    ) * HEAD_DIM ** (-0.5)


def backward_all(queries, key_rows, value_rows, totals, context, grad_context):
    results = []
    for sample in range(queries.shape[0]):
        grad_rows = backward_attend(
            split_heads(queries[sample]),
            split_heads(key_rows[sample]),
            split_heads(value_rows[sample]),
            totals[sample],
            split_heads(context[sample]),
            split_heads(grad_context[sample]),
        )
        results.append(grad_rows.reshape(queries.shape[1], queries.shape[2]))
    return jnp.stack(results).astype(jnp.bfloat16)


def per_device(series, target, w_embed, w_query, w_key, w_value, w_out, norm_gain, w_head):
    samples, var_rows, steps_local = series.shape
    look_total = steps_local * lax.axis_size("tm")
    series_f = series.astype(jnp.float32)
    level_sum, square_sum = lax.psum(
        (jnp.sum(series_f, axis=2), jnp.sum(series_f * series_f, axis=2)), "tm"
    )
    instance_average = level_sum / look_total
    spread = square_sum / look_total - instance_average * instance_average
    centered = series_f - instance_average[:, :, None]
    instance_dispersion = jnp.sqrt(spread + epsilon)
    normed = (centered / instance_dispersion[:, :, None]).astype(jnp.bfloat16)
    partial_embed = jnp.einsum("svl,ld->svd", normed, w_embed, preferred_element_type=jnp.float32)
    hidden = lax.psum(partial_embed, "tm").astype(jnp.bfloat16)
    queries = project(hidden, w_query)
    key_rows = project(hidden, w_key)
    value_rows = project(hidden, w_value)
    all_keys, all_values = (
        lax.all_gather(key_rows, "var", axis=1, tiled=True),
        lax.all_gather(value_rows, "var", axis=1, tiled=True),
    )
    context, totals = attend_all(queries, all_keys, all_values)
    context_low = context.astype(jnp.bfloat16)
    mixing = lax.psum(
        jnp.einsum("sva,ad->svd", context_low, w_out, preferred_element_type=jnp.float32).astype(
            jnp.bfloat16
        ),
        "tm",
    ).astype(jnp.float32)
    residual = hidden.astype(jnp.float32) + mixing
    shifted = residual - jnp.mean(residual, axis=2, keepdims=True)
    norm_root = jnp.sqrt(jnp.mean(shifted * shifted, axis=2, keepdims=True) + epsilon)
    unit_rows = shifted / norm_root
    normal_out = (unit_rows * norm_gain).astype(jnp.bfloat16)
    future_rescaler = jnp.einsum(
        "svd,dh->svh", normal_out, w_head, preferred_element_type=jnp.float32
    )
    predicted_values = (
        future_rescaler * instance_dispersion[:, :, None] + instance_average[:, :, None]
    )
    errors = (
        future_rescaler - (target - instance_average[:, :, None]) / instance_dispersion[:, :, None]
    )
    grad_horizon = (errors * (2.0 / (SAMPLES * HOR))).astype(jnp.bfloat16)
    head_term = jnp.einsum(
        "svd,svh->dh", normal_out, grad_horizon, preferred_element_type=jnp.float32
    )
    grad_normal = lax.psum(
        jnp.einsum("svh,dh->svd", grad_horizon, w_head, preferred_element_type=jnp.float32).astype(
            jnp.bfloat16
        ),
        "tm",
    ).astype(jnp.float32)
    gain_term = jnp.sum(grad_normal * unit_rows, axis=(0, 1))
    grad_unit = grad_normal * norm_gain
    grad_mix = (
        (
            grad_unit
            - jnp.mean(grad_unit, axis=2, keepdims=True)
            - unit_rows * jnp.mean(grad_unit * unit_rows, axis=2, keepdims=True)
        )
        / norm_root
    ).astype(jnp.bfloat16)
    out_term = jnp.einsum("sva,svd->da", context_low, grad_mix, preferred_element_type=jnp.float32)
    grad_context = jnp.einsum("svd,ad->sva", grad_mix, w_out, preferred_element_type=jnp.float32)
    grad_query = backward_all(queries, all_keys, all_values, totals, context, grad_context)
    query_term = jnp.einsum("svd,sva->da", hidden, grad_query, preferred_element_type=jnp.float32)
    future_readout_derivative, gain_gradient_total, output_gradient_total, query_gradient_total = (
        lax.psum((head_term, gain_term, out_term, query_term), "var")
    )
    return (
        predicted_values,
        query_gradient_total,
        jnp.transpose(output_gradient_total),
        gain_gradient_total,
        future_readout_derivative,
    )


def solution(mesh):
    in_specs = (
        P("groups", "var", "tm"),
        P("groups", "var", "tm"),
        P("tm", None),
        P(None, "tm"),
        P(None, "tm"),
        P(None, "tm"),
        P("tm", None),
        P(),
        P(None, "tm"),
    )
    out_specs = (
        P("groups", "var", "tm"),
        P("groups", "tm"),
        P(("groups", "tm"), None),
        P("groups"),
        P("groups", "tm"),
    )
    return jax.shard_map(
        per_device, mesh=mesh, in_specs=in_specs, out_specs=out_specs, check_vma=False
    )
```

profile of v0, /device:TPU:0, one launch (start us, length us, event | category | flops | bytes accessed | tf_op | source)
XLA Modules:
  0.0 234.3 jit_solution(17725710917691183952)
XLA Ops:
  7.2 1.4 convert_reduce_fusion
  8.6 2.6 %all-reduce.1 = (f32[2,64]{1,0:T(2,128)S(1)}, f32[2,64]{1,0:T(2,128)S(1)}) all-reduce(f32[2,64]{1,0:T(2,128)S(1)} %get-tuple-element.6, f32[2,64]{1,0:T(2,128)S(1)} %get-tuple-element.5), channel_id=1, replica_groups=mesh['groups'=2,'var'=8,'tm'=2] {'tm'}, use_global_device_ids=true, to_apply=%region_3.0 | all-reduce | flops 256 | bytes 2048 | tf_op jit(solution)/shard_map/psum | solution.py:87
  11.2 0.6 copy-done.16
  11.8 1.6 fusion
  13.4 4.4 %all-reduce.12 = bf16[2,64,512]{2,1,0:T(8,128)(2,1)S(1)} all-reduce(f32[2,64,512]{2,1,0:T(8,128)S(1)} %fusion), channel_id=1, replica_groups=mesh['groups'=2,'var'=8,'tm'=2] {'tm'}, use_global_device_ids=true, to_apply=%region_4.0 | all-reduce | flops 65536 | bytes 393216 | tf_op jit(solution)/shard_map/psum | solution.py:96
  17.8 0.2 convolution_convert_fusion.2
  18.0 0.2 convolution_convert_fusion.3
  18.2 0.1 reshape_squeeze.31
  18.3 0.1 reshape_squeeze.34
  18.3 0.2 convolution_convert_fusion.4
  18.5 32.3 %all_gather.6 = bf16[2,512,128]{2,1,0:T(8,128)(2,1)S(1)} all-gather(bf16[2,64,128]{2,1,0:T(8,128)(2,1)S(1)} %convolution_convert_fusion.4), channel_id=1, replica_groups=mesh['groups'=2,'var'=8,'tm'=2] {'var'}, dimensions={1}, use_global_device_ids=true | all-gather | bytes 294912 | tf_op jit(solution)/shard_map/all_gather | solution.py:102
  50.9 0.1 copy.28
  51.0 0.1 copy.31
  51.1 30.7 %all_gather.7 = bf16[2,512,128]{2,1,0:T(8,128)(2,1)S(1)} all-gather(bf16[2,64,128]{2,1,0:T(8,128)(2,1)S(1)} %convolution_convert_fusion.2), channel_id=1, replica_groups=mesh['groups'=2,'var'=8,'tm'=2] {'var'}, dimensions={1}, use_global_device_ids=true | all-gather | bytes 294912 | tf_op jit(solution)/shard_map/all_gather | solution.py:101
  81.9 0.1 copy.29
  82.0 0.1 copy.32
  82.1 0.3 fusion.68
  82.4 0.8 fusion.69
  83.2 0.1 copy.35
  83.3 0.3 fusion.70
  83.5 0.8 fusion.71
  84.3 0.1 copy.34
  84.5 0.8 convolution_convert_fusion.1
  85.4 18.9 %all-reduce.7.cloned.1.call-done = bf16[2,64,512]{2,1,0:T(8,128)(2,1)} async-done(((bf16[2,64,512]{2,1,0:T(8,128)(2,1)}), bf16[2,64,512]{2,1,0:T(8,128)(2,1)}) %all-reduce.7.cloned.1.call-update) | async-done | bytes 131088 | tf_op jit(solution)/shard_map/psum | solution.py:106
  104.3 1.1 fusion.36
  105.4 1.1 multiply_reduce_fusion
  106.5 2.2 multiply_convert_fusion.1
  108.7 0.6 copy-done.9
  109.3 0.9 convolution_convert_fusion
  110.3 2.1 convolution_bitcast_fusion
  112.4 17.0 %all-reduce.9.cloned.1.call-done = bf16[2,64,512]{2,1,0:T(8,128)(2,1)} async-done(((bf16[2,64,512]{2,1,0:T(8,128)(2,1)}), bf16[2,64,512]{2,1,0:T(8,128)(2,1)}) %all-reduce.9.cloned.1.call-update) | async-done | bytes 131088 | tf_op jit(solution)/shard_map/psum | solution.py:130
  129.5 1.7 fusion.31
  131.2 1.1 fusion.34
  132.3 0.2 fusion.38
  132.5 1.6 convolution_bitcast_fusion.1
  134.1 0.1 copy.36
  134.2 0.9 multiply_reduce_fusion.2
  135.1 1.1 fusion.15
  136.2 0.1 copy.38
  136.3 0.1 copy.37
  136.4 0.4 fusion.14
  136.8 0.1 copy.39
  136.9 0.9 convolution_bitcast_fusion.2
  137.9 22.8 %psum.70 = f32[512]{0:T(512)} all-reduce(f32[512]{0:T(512)S(1)} %copy-done.12), channel_id=1, replica_groups=mesh['groups'=2,'var'=8,'tm'=2] {'var'}, use_global_device_ids=true, to_apply=%region_18.0 | all-reduce | flops 512 | bytes 4096 | tf_op jit(solution)/shard_map/psum | solution.py:151
  160.6 61.8 %all-reduce.11.cloned.1.call-done = (f32[512,128]{1,0:T(8,128)}, f32[128,512]{1,0:T(8,128)}, f32[512,360]{0,1:T(8,128)}) async-done(((f32[512,128]{1,0:T(8,128)}, f32[128,512]{1,0:T(8,128)}, f32[512,360]{0,1:T(8,128)}), (f32[512,128]{1,0:T(8,128)}, f32[128,512]{1,0:T(8,128)}, f32[512,360]{0,1:T(8,128)})) %all-reduce.11.cloned.1.call-update) | async-done | bytes 1261584 | tf_op jit(solution)/shard_map/psum | solution.py:151
  222.4 1.7 copy.55
  224.0 1.7 copy.56
  225.7 2.0 copy.57
  (49 shorter events, 0.4 us)
Async XLA Ops:
  7.2 4.6 %copy-start = (bf16[2048,512]{1,0:T(8,128)(2,1)S(1)}, bf16[2048,512]{1,0:T(8,128)(2,1)}, u32[]{:S(2)}) copy-start(bf16[2048,512]{1,0:T(8,128)(2,1)} %param.11) | copy-start | bytes 6291460
  7.2 97.1 %all-reduce.7.cloned.1.call-start = ((), (), s32[]{:S(2)}) async-start(), calls=%async_computation | async-start | bytes 262144 | tf_op jit(solution)/shard_map/psum | solution.py:106
  11.2 0.6 copy-start.16
  11.2 0.6 copy-start.17
  11.8 6.0 %copy-start.6 = (bf16[512,128]{1,0:T(8,128)(2,1)S(1)}, bf16[512,128]{1,0:T(8,128)(2,1)}, u32[]{:S(2)}) copy-start(bf16[512,128]{1,0:T(8,128)(2,1)} %param.13) | copy-start | bytes 393220
  11.8 6.2 %copy-start.7 = (bf16[512,128]{1,0:T(8,128)(2,1)S(1)}, bf16[512,128]{1,0:T(8,128)(2,1)}, u32[]{:S(2)}) copy-start(bf16[512,128]{1,0:T(8,128)(2,1)} %param.12) | copy-start | bytes 393220
  11.8 6.5 %copy-start.8 = (bf16[512,128]{1,0:T(8,128)(2,1)S(1)}, bf16[512,128]{1,0:T(8,128)(2,1)}, u32[]{:S(2)}) copy-start(bf16[512,128]{1,0:T(8,128)(2,1)} %param.14) | copy-start | bytes 393220
  50.8 33.6 %copy-start.2 = (bf16[128,512]{1,0:T(8,128)(2,1)S(1)}, bf16[128,512]{1,0:T(8,128)(2,1)}, u32[]{:S(2)}) copy-start(bf16[128,512]{1,0:T(8,128)(2,1)} %param.15) | copy-start | bytes 393220
  82.4 0.9 copy-start.13
  83.5 1.8 copy-start.15
  84.4 0.9 copy-start.5
  85.3 44.2 %all-reduce.9.cloned.1.call-start = ((), (), s32[]{:S(2)}) async-start(), calls=%async_computation.1 | async-start | bytes 262144 | tf_op jit(solution)/shard_map/psum | solution.py:130
  104.3 5.0 %copy-start.3 = (bf16[512,360]{0,1:T(8,128)(2,1)S(1)}, bf16[512,360]{0,1:T(8,128)(2,1)}, u32[]{:S(2)}) copy-start(bf16[512,360]{0,1:T(8,128)(2,1)} %param.17) | copy-start | bytes 1105924
  104.3 6.0 %copy-start.1 = (bf16[2,64,512]{2,1,0:T(8,128)(2,1)S(1)}, bf16[2,64,512]{2,1,0:T(8,128)(2,1)}, u32[]{:S(2)}) copy-start(bf16[2,64,512]{2,1,0:T(8,128)(2,1)} %all-reduce.7.cloned.1.call-done) | copy-start | bytes 393220
  105.4 1.1 copy-start.10
  106.5 2.2 copy-start.11
  108.7 0.6 copy-start.9
  110.2 112.1 %all-reduce.11.cloned.1.call-start = ((), (), s32[]{:S(2)}) async-start(), calls=%async_computation.2 | async-start | bytes 2523136 | tf_op jit(solution)/shard_map/psum | solution.py:151
  132.3 4.1 %copy-start.4 = (f32[64,2,64]{0,2,1:T(8,128)S(1)}, f32[64,2,64]{0,2,1:T(8,128)}, u32[]{:S(2)}) copy-start(f32[64,2,64]{0,2,1:T(8,128)} %get-tuple-element.30) | copy-start | bytes 98308
  132.3 4.1 %copy-start.14 = (f32[2,64]{1,0:T(2,128)S(1)}, f32[2,64]{1,0:T(2,128)}, u32[]{:S(2)}) copy-start(f32[2,64]{1,0:T(2,128)} %copy-done.13) | copy-start | bytes 1540
  135.1 2.8 %copy-start.12 = (f32[512]{0:T(512)S(1)}, f32[512]{0:T(512)}, u32[]{:S(2)}) copy-start(f32[512]{0:T(512)} %get-tuple-element.7) | copy-start | bytes 6148
Sparse Core Ops, SparseCore 0:
  85.4 18.8 all-reduce.6
  110.4 19.0 all-reduce.8
  138.0 84.3 all-reduce.10
where the time goes:
time: 235 us; the launch traced here: 234 us
  waiting for transfers between devices  97.8 us (42%)
  blocking collectives  92.8 us (39%)
  matrix products  14.4 us (6%)
  between operations  14.1 us (6%)
  local copies, waits for them, and re-layouts  7.82 us (3%)
  other arithmetic  7.29 us (3%)
    psum x1, waiting for transfers between devices, per_device(): lax.psum((head_term, gain_term, out_term, query_term), 'var')  61.8 us
    all_gather x1, blocking collectives, per_device(): lax.all_gather(value_rows, 'var', axis=1, tiled=True)  32.3 us
    all_gather x1, blocking collectives, per_device(): lax.all_gather(key_rows, 'var', axis=1, tiled=True)  30.7 us
    psum x1, blocking collectives, per_device(): lax.psum((head_term, gain_term, out_term, query_term), 'var')  22.8 us
    psum x1, waiting for transfers between devices, per_device(): lax.psum(jnp.einsum('sva,ad->svd', context_low, w_out, preferred_element_...  18.9 us
    psum x1, waiting for transfers between devices, per_device(): lax.psum(jnp.einsum('svh,dh->svd', grad_horizon, w_head, preferred_elemen...  17 us
    unnamed x39, local copies, waits for them, and re-layouts  6.63 us
  transfers between devices with their start and end apart: 3, of which 3 were waited for; matrix products, arithmetic and copies ran while one was open for 1% of the time, Pallas kernels for 0%

commit v1 on v0

--- a/solution.py
+++ b/solution.py
@@ -127,11 +127,14 @@
     head_term = jnp.einsum(
         "svd,svh->dh", normal_out, grad_horizon, preferred_element_type=jnp.float32
     )
-    grad_normal = lax.psum(
-        jnp.einsum("svh,dh->svd", grad_horizon, w_head, preferred_element_type=jnp.float32).astype(
-            jnp.bfloat16
+    grad_normal = jnp.sum(
+        lax.all_gather(
+            jnp.einsum(
+                "svh,dh->svd", grad_horizon, w_head, preferred_element_type=jnp.float32
+            ).astype(jnp.bfloat16),
+            "tm",
         ),
-        "tm",
+        0,
     ).astype(jnp.float32)
     gain_term = jnp.sum(grad_normal * unit_rows, axis=(0, 1))
     grad_unit = grad_normal * norm_gain

time: 235 us -> 218 us (0.928)
  waiting for transfers between devices: 97.8 us -> 80.7 us
    psum x1 -> x0, waiting for transfers between devices: 17 us -> none  [per_device(): lax.psum(jnp.einsum('svh,dh->svd', grad_horizon, w_head, preferred_elemen...]
    unnamed x39 -> x49, local copies, waits for them, and re-layouts: 6.63 us -> 6.09 us
  transfers between devices with their start and end apart: 3 -> 2, of which waited for: 3 -> 2; matrix products, arithmetic and copies ran while one was open for 1% -> 0% of each run, Pallas kernels for 0% -> 0%
where the time goes in v1:
time: 218 us
  blocking collectives  94.9 us (44%)
  waiting for transfers between devices  80.7 us (37%)
  between operations  14.5 us (7%)
  matrix products  13.9 us (6%)
  local copies, waits for them, and re-layouts  7.29 us (3%)
  other arithmetic  6.4 us (3%)
    psum x1, waiting for transfers between devices, per_device(): lax.psum((head_term, gain_term, out_term, query_term), 'var')  61.8 us
    all_gather x1, blocking collectives, per_device(): lax.all_gather(value_rows, 'var', axis=1, tiled=True)  32.3 us
    all_gather x1, blocking collectives, per_device(): lax.all_gather(key_rows, 'var', axis=1, tiled=True)  30.9 us
    psum x1, blocking collectives, per_device(): lax.psum((head_term, gain_term, out_term, query_term), 'var')  22.7 us
    psum x1, waiting for transfers between devices, per_device(): lax.psum(jnp.einsum('sva,ad->svd', context_low, w_out, preferred_element_...  18.8 us
    unnamed x49, local copies, waits for them, and re-layouts  6.09 us
  transfers between devices with their start and end apart: 2, of which 2 were waited for; matrix products, arithmetic and copies ran while one was open for 0% of the time, Pallas kernels for 0%

profile of v1, /device:TPU:0, one launch (start us, length us, event | category | flops | bytes accessed | tf_op | source)
XLA Modules:
  0.0 217.7 jit_solution(7303542440859938488)
XLA Ops:
  7.2 1.4 convert_reduce_fusion
  8.6 2.6 %all-reduce.1 = (f32[2,64]{1,0:T(2,128)S(1)}, f32[2,64]{1,0:T(2,128)S(1)}) all-reduce(f32[2,64]{1,0:T(2,128)S(1)} %get-tuple-element.6, f32[2,64]{1,0:T(2,128)S(1)} %get-tuple-element.5), channel_id=1, replica_groups=mesh['groups'=2,'var'=8,'tm'=2] {'tm'}, use_global_device_ids=true, to_apply=%region_3.0 | all-reduce | flops 256 | bytes 2048 | tf_op jit(solution)/shard_map/psum | solution.py:87
  11.3 1.6 fusion
  12.9 4.4 %all-reduce.9 = bf16[2,64,512]{2,1,0:T(8,128)(2,1)S(1)} all-reduce(f32[2,64,512]{2,1,0:T(8,128)S(1)} %fusion), channel_id=1, replica_groups=mesh['groups'=2,'var'=8,'tm'=2] {'tm'}, use_global_device_ids=true, to_apply=%region_4.0 | all-reduce | flops 65536 | bytes 393216 | tf_op jit(solution)/shard_map/psum | solution.py:96
  17.2 0.2 convolution_convert_fusion.2
  17.4 0.2 convolution_convert_fusion.3
  17.6 0.1 reshape_squeeze.31
  17.7 0.1 reshape_squeeze.34
  17.8 0.2 convolution_convert_fusion.4
  18.0 32.3 %all_gather.12 = bf16[2,512,128]{2,1,0:T(8,128)(2,1)S(1)} all-gather(bf16[2,64,128]{2,1,0:T(8,128)(2,1)S(1)} %convolution_convert_fusion.4), channel_id=1, replica_groups=mesh['groups'=2,'var'=8,'tm'=2] {'var'}, dimensions={1}, use_global_device_ids=true | all-gather | bytes 294912 | tf_op jit(solution)/shard_map/all_gather | solution.py:102
  50.3 0.1 copy.40
  50.5 0.1 copy.43
  50.6 30.9 %all_gather.13 = bf16[2,512,128]{2,1,0:T(8,128)(2,1)S(1)} all-gather(bf16[2,64,128]{2,1,0:T(8,128)(2,1)S(1)} %convolution_convert_fusion.2), channel_id=1, replica_groups=mesh['groups'=2,'var'=8,'tm'=2] {'var'}, dimensions={1}, use_global_device_ids=true | all-gather | bytes 294912 | tf_op jit(solution)/shard_map/all_gather | solution.py:101
  81.5 0.1 copy.41
  81.6 0.1 copy.44
  81.7 0.3 fusion.68
  82.0 0.8 fusion.69
  82.8 0.1 copy.47
  82.9 0.3 fusion.70
  83.2 0.8 fusion.71
  84.0 0.1 copy.46
  84.1 0.8 convolution_convert_fusion.1
  84.9 0.0 all-reduce.8.cloned.1.call-start
  85.0 18.8 %all-reduce.6.cloned.1.call-done = bf16[2,64,512]{2,1,0:T(8,128)(2,1)} async-done(((bf16[2,64,512]{2,1,0:T(8,128)(2,1)}), bf16[2,64,512]{2,1,0:T(8,128)(2,1)}) %all-reduce.6.cloned.1.call-update) | async-done | bytes 131088 | tf_op jit(solution)/shard_map/psum | solution.py:106
  103.8 1.1 fusion.36
  104.9 1.1 multiply_reduce_fusion
  106.1 2.1 multiply_convert_fusion.1
  108.2 0.6 copy-done.13
  108.8 0.2 convolution_convert_fusion
  109.1 2.0 all-gather
  111.2 1.0 fusion.31
  112.2 0.8 fusion.34
  113.1 0.2 fusion.38
  113.2 1.6 convolution_bitcast_fusion.1
  114.9 0.1 copy.48
  115.0 0.9 multiply_reduce_fusion.2
  115.8 1.3 fusion.15
  117.2 0.1 copy.52
  117.3 0.1 copy.50
  117.5 0.4 fusion.14
  117.8 0.1 copy.53
  117.9 0.9 convolution_bitcast_fusion.2
  118.9 2.1 convolution_bitcast_fusion
  121.0 22.7 %psum.62 = f32[512]{0:T(512)} all-reduce(f32[512]{0:T(512)S(1)} %get-tuple-element.7), channel_id=1, replica_groups=mesh['groups'=2,'var'=8,'tm'=2] {'var'}, use_global_device_ids=true, to_apply=%region_18.0 | all-reduce | flops 512 | bytes 4096 | tf_op jit(solution)/shard_map/psum | solution.py:154
  143.7 61.8 %all-reduce.8.cloned.1.call-done = (f32[512,128]{1,0:T(8,128)}, f32[128,512]{1,0:T(8,128)}, f32[512,360]{0,1:T(8,128)}) async-done(((f32[512,128]{1,0:T(8,128)}, f32[128,512]{1,0:T(8,128)}, f32[512,360]{0,1:T(8,128)}), (f32[512,128]{1,0:T(8,128)}, f32[128,512]{1,0:T(8,128)}, f32[512,360]{0,1:T(8,128)})) %all-reduce.8.cloned.1.call-update) | async-done | bytes 1261584 | tf_op jit(solution)/shard_map/psum | solution.py:154
  205.5 1.7 copy.70
  207.2 1.7 copy.71
  208.9 2.0 copy.72
  (58 shorter events, 0.3 us)
Async XLA Ops:
  7.2 4.1 %copy-start = (bf16[2048,512]{1,0:T(8,128)(2,1)S(1)}, bf16[2048,512]{1,0:T(8,128)(2,1)}, u32[]{:S(2)}) copy-start(bf16[2048,512]{1,0:T(8,128)(2,1)} %param.11) | copy-start | bytes 6291460
  7.2 96.6 %all-reduce.6.cloned.1.call-start = ((), (), s32[]{:S(2)}) async-start(), calls=%async_computation | async-start | bytes 262144 | tf_op jit(solution)/shard_map/psum | solution.py:106
  11.2 6.0 %copy-start.10 = (bf16[512,128]{1,0:T(8,128)(2,1)S(1)}, bf16[512,128]{1,0:T(8,128)(2,1)}, u32[]{:S(2)}) copy-start(bf16[512,128]{1,0:T(8,128)(2,1)} %param.13) | copy-start | bytes 393220
  11.2 6.2 %copy-start.11 = (bf16[512,128]{1,0:T(8,128)(2,1)S(1)}, bf16[512,128]{1,0:T(8,128)(2,1)}, u32[]{:S(2)}) copy-start(bf16[512,128]{1,0:T(8,128)(2,1)} %param.12) | copy-start | bytes 393220
  11.3 6.5 %copy-start.12 = (bf16[512,128]{1,0:T(8,128)(2,1)S(1)}, bf16[512,128]{1,0:T(8,128)(2,1)}, u32[]{:S(2)}) copy-start(bf16[512,128]{1,0:T(8,128)(2,1)} %param.14) | copy-start | bytes 393220
  50.3 33.8 %copy-start.2 = (bf16[128,512]{1,0:T(8,128)(2,1)S(1)}, bf16[128,512]{1,0:T(8,128)(2,1)}, u32[]{:S(2)}) copy-start(bf16[128,512]{1,0:T(8,128)(2,1)} %param.15) | copy-start | bytes 393220
  50.4 57.8 %copy-start.6 = (bf16[1,512,128]{1,2,0:T(8,128)(2,1)}, bf16[1,512,128]{1,2,0:T(8,128)(2,1)S(1)}, u32[]{:S(2)}) copy-start(bf16[1,512,128]{1,2,0:T(8,128)(2,1)S(1)} %copy.40) | copy-start | bytes 393220
  50.6 32.3 %copy-start.4 = (bf16[1,512,128]{1,2,0:T(8,128)(2,1)}, bf16[1,512,128]{1,2,0:T(8,128)(2,1)S(1)}, u32[]{:S(2)}) copy-start(bf16[1,512,128]{1,2,0:T(8,128)(2,1)S(1)} %copy.43) | copy-start | bytes 393220
  50.6 55.5 %copy-start.18 = (f32[512]{0:T(512)S(1)}, f32[512]{0:T(512)}, u32[]{:S(2)}) copy-start(f32[512]{0:T(512)} %param.16) | copy-start | bytes 6148
  81.6 22.2 %copy-start.3 = (bf16[1,512,128]{1,2,0:T(8,128)(2,1)}, bf16[1,512,128]{1,2,0:T(8,128)(2,1)S(1)}, u32[]{:S(2)}) copy-start(bf16[1,512,128]{1,2,0:T(8,128)(2,1)S(1)} %copy.41) | copy-start | bytes 393220
  82.0 24.1 %copy-start.20 = (f32[2,64]{1,0:T(2,128)}, f32[2,64]{1,0:T(2,128)S(1)}, u32[]{:S(2)}) copy-start(f32[2,64]{1,0:T(2,128)S(1)} %get-tuple-element.27) | copy-start | bytes 1540
  83.2 22.9 %copy-start.22 = (f32[2,64]{1,0:T(2,128)}, f32[2,64]{1,0:T(2,128)S(1)}, u32[]{:S(2)}) copy-start(f32[2,64]{1,0:T(2,128)S(1)} %get-tuple-element.31) | copy-start | bytes 1540
  84.1 24.1 %copy-start.9 = (bf16[1,64,128]{2,1,0:T(8,128)(2,1)}, bf16[1,64,128]{2,1,0:T(8,128)(2,1)S(1)}, u32[]{:S(2)}) copy-start(bf16[1,64,128]{2,1,0:T(8,128)(2,1)S(1)} %copy.46) | copy-start | bytes 49156
  84.9 120.6 %all-reduce.8.cloned.1.call-start = ((), (), s32[]{:S(2)}) async-start(), calls=%async_computation.1 | async-start | bytes 2523136 | tf_op jit(solution)/shard_map/psum | solution.py:154
  103.8 5.0 %copy-start.7 = (bf16[512,360]{0,1:T(8,128)(2,1)S(1)}, bf16[512,360]{0,1:T(8,128)(2,1)}, u32[]{:S(2)}) copy-start(bf16[512,360]{0,1:T(8,128)(2,1)} %param.17) | copy-start | bytes 1105924
  104.9 6.2 %copy-start.1 = (bf16[2,64,512]{2,1,0:T(8,128)(2,1)S(1)}, bf16[2,64,512]{2,1,0:T(8,128)(2,1)}, u32[]{:S(2)}) copy-start(bf16[2,64,512]{2,1,0:T(8,128)(2,1)} %all-reduce.6.cloned.1.call-done) | copy-start | bytes 393220
  104.9 3.3 %copy-start.14 = (f32[2,64]{1,0:T(2,128)}, f32[2,64]{1,0:T(2,128)S(1)}, u32[]{:S(2)}) copy-start(f32[2,64]{1,0:T(2,128)S(1)} %broadcast_multiply_fusion.2) | copy-start | bytes 1540
  106.1 2.1 copy-start.16
  108.2 0.6 copy-start.13
  111.1 6.3 %copy-start.8 = (f32[64,2,64]{0,2,1:T(8,128)S(1)}, f32[64,2,64]{0,2,1:T(8,128)}, u32[]{:S(2)}) copy-start(f32[64,2,64]{0,2,1:T(8,128)} %get-tuple-element.30) | copy-start | bytes 98308
  111.1 6.3 %copy-start.5 = (bf16[1,512,128]{1,2,0:T(8,128)(2,1)S(1)}, bf16[1,512,128]{1,2,0:T(8,128)(2,1)}, u32[]{:S(2)}) copy-start(bf16[1,512,128]{1,2,0:T(8,128)(2,1)} %copy-done.4) | copy-start | bytes 393220
  111.2 6.3 %copy-start.21 = (f32[2,64]{1,0:T(2,128)S(1)}, f32[2,64]{1,0:T(2,128)}, u32[]{:S(2)}) copy-start(f32[2,64]{1,0:T(2,128)} %copy-done.20) | copy-start | bytes 1540
  113.0 5.9 %copy-start.15 = (f32[2,64]{1,0:T(2,128)S(1)}, f32[2,64]{1,0:T(2,128)}, u32[]{:S(2)}) copy-start(f32[2,64]{1,0:T(2,128)} %copy-done.14) | copy-start | bytes 1540
  113.0 5.8 %copy-start.17 = (f32[2,64]{1,0:T(2,128)S(1)}, f32[2,64]{1,0:T(2,128)}, u32[]{:S(2)}) copy-start(f32[2,64]{1,0:T(2,128)} %copy-done.16) | copy-start | bytes 1540
  113.0 5.8 %copy-start.19 = (f32[512]{0:T(512)S(1)}, f32[512]{0:T(512)}, u32[]{:S(2)}) copy-start(f32[512]{0:T(512)} %param.16) | copy-start | bytes 6148
Sparse Core Ops, SparseCore 0:
  85.1 18.7 all-reduce.5
  121.1 84.3 all-reduce.7
